TPU v7x, 512 devices: a whole 4x8x8 slice. The times are simulated.
512 devices in a mesh: bucket: 128 (over x, z_lo, y), rel: 4 (over z_hi, core).
Axes of the slice: x: 4, y: 8, z: 8 (z_hi: 2, z_lo: 4; z = z_hi * 4 + z_lo), core: 2. Of those that a mesh axis runs over, the one named last changes fastest.
Arguments:
- src_feat: bfloat16 [32768, 768], P(('bucket', 'rel')), may hold values from -22 to 22
- tgt_feat: bfloat16 [65536, 768], P(('bucket', 'rel')), may hold values from -22 to 22
- enc_weight: bfloat16 [768, 512], replicated, may hold values from -0.21875 to 0.21875
- rel_shift: bfloat16 [12, 512], P('rel'), may hold values from -3 to 3
- edge_src: int32 [128, 4, 4, 768], P('bucket', 'rel'), may hold values from 0 to 255
- edge_tgt: int32 [128, 4, 4, 768], P('bucket', 'rel'), may hold values from 0 to 511
- rel_hot: int32 [128, 4, 4, 3, 768], P('bucket', 'rel'), may hold values from 0 to 1, as said below
- neg_idx: int32 [128, 4, 4, 128], P('bucket', 'rel'), may hold values from 0 to 511
- edge_label: int32 [128, 4, 4, 768], P('bucket', 'rel'), may hold values 0 or 1
Outputs:
- src_grad: float32 [32768, 512], P(('bucket', 'rel'))
- tgt_grad: float32 [65536, 512], P(('bucket', 'rel'))
- rel_grad: float32 [12, 512], P('rel')
- enc_grad: float32 [768, 512], replicated
Inputs may be any that keep to these rules, and one draw needn't show every extreme that they name: `rel_hot`: for each edge exactly one of the three entries is 1.
All inputs are finite; a program needn't handle non-finite values. No bound on the sum of `edge_label` on one device may be relied on, other than what follows from the above.
Results may differ from a plain program's by a relative error of at most 0.00065.
The roundings to bfloat16 on the way count: a program that leaves them out, or rounds other values in their place, can miss the bound.
Values may be sent and summed in bfloat16 or wider, within the bound.
A program may use at most 64 MiB of HBM per device.

v0:
```python
import jax
import jax.numpy as jnp
from jax import lax
from jax.experimental import pallas as pl
from jax.experimental.pallas import tpu as pltpu
from jax.sharding import PartitionSpec as P

EMB = 512
NEG = 128
MEETS = 4
F32 = jnp.float32
BF16 = jnp.bfloat16
MESH = pl.DeviceIdType.MESH
AXIS = {"x": 4, "y": 8, "z": 8}
HALF = 224
PARTS = (("z", "y", "x", 0, 64), ("y", "z", "x", 64, 64), ("x", "y", "z", 128, 96))


class Place:
    def __init__(self):
        b, q = lax.axis_index("bucket"), lax.axis_index("rel")
        self.at = {
            "x": lax.div(b, 32),
            "y": lax.rem(b, 8),
            "z": lax.div(q, 2) * 4 + lax.rem(lax.div(b, 8), 4),
            "k": lax.rem(q, 2),
        }

    def device(self, **moved):
        at = dict(self.at, **moved)
        bucket = at["x"] * 32 + lax.rem(at["z"], 4) * 8 + at["y"]
        return bucket, lax.div(at["z"], 4) * 2 + at["k"]

    def along(self, axis, apart):
        there = lax.rem(self.at[axis] + apart, AXIS[axis])
        return there, self.device(**{axis: there})

    def other_core(self):
        return self.device(k=1 - self.at["k"])


class Wires:
    def __init__(self, send_sems, recv_sems):
        self.send_sems, self.recv_sems, self.used, self.open = send_sems, recv_sems, 0, []

    def send(self, src, dst, device):
        copy = pltpu.make_async_remote_copy(
            src_ref=src,
            dst_ref=dst,
            send_sem=self.send_sems.at[self.used],
            recv_sem=self.recv_sems.at[self.used],
            device_id=device,
            device_id_type=MESH,
        )
        copy.start()
        self.used += 1
        self.open.append(copy)
        return copy

    def finish(self):
        for copy in self.open:
            copy.wait_send()


def reduce_everywhere(place, wires, local, pair, mine, full, firsts, seconds, thirds, sums1, sums2):
    at, k = place.at, place.at["k"]
    other = place.other_core()
    copies = []
    for _, _, _, base, size in PARTS:
        size = min(size, 196 - base)
        copies.append(
            wires.send(local.at[pl.ds((1 - k) * HALF + base, size)], pair.at[pl.ds(base, size)], other)
        )
    mine[pl.ds(196, 28)] = jnp.zeros((28, 8, 128), F32)
    pending1 = []
    for p, (first, _, _, base, size) in enumerate(PARTS):
        copies[p].wait_recv()
        real = min(size, 196 - base)
        mine[pl.ds(base, real)] = local[pl.ds(k * HALF + base, real)] + pair[pl.ds(base, real)]
        block = size // AXIS[first]
        here = []
        for apart in range(1, AXIS[first]):
            there, device = place.along(first, apart)
            here.append(
                wires.send(mine.at[pl.ds(base + there * block, block)], firsts[p].at[apart], device)
            )
        pending1.append(here)
    pending2 = []
    for p, (first, second, _, base, size) in enumerate(PARTS):
        block = size // AXIS[first]
        total = mine[pl.ds(base + at[first] * block, block)]
        for apart in range(1, AXIS[first]):
            pending1[p][apart - 1].wait_recv()
            total = total + firsts[p][apart]
        sums1[p][...] = total
        small = block // AXIS[second]
        here = []
        for apart in range(1, AXIS[second]):
            there, device = place.along(second, apart)
            here.append(
                wires.send(sums1[p].at[pl.ds(there * small, small)], seconds[p].at[apart], device)
            )
        pending2.append(here)
    pending3 = []
    for p, (first, second, third, base, size) in enumerate(PARTS):
        small = size // AXIS[first] // AXIS[second]
        total = sums1[p][pl.ds(at[second] * small, small)]
        for apart in range(1, AXIS[second]):
            pending2[p][apart - 1].wait_recv()
            total = total + seconds[p][apart]
        sums2[p][...] = total
        here = []
        for apart in range(1, AXIS[third]):
            here.append(wires.send(sums2[p], thirds[p].at[apart], place.along(third, apart)[1]))
        pending3.append(here)
    pending4 = []
    for p, (first, second, third, base, size) in enumerate(PARTS):
        thirds[p][0] = sums2[p][...]
        for apart in range(1, AXIS[third]):
            pending3[p][apart - 1].wait_recv()
        total = 0.0
        for where in range(AXIS[third]):
            total = total + thirds[p][lax.rem(at[third] + AXIS[third] - where, AXIS[third])]
        block = size // AXIS[first]
        small = block // AXIS[second]
        own = k * HALF + base + at[first] * block + at[second] * small
        full[pl.ds(own, small)] = total
        here = []
        for apart in range(1, AXIS[second]):
            piece = full.at[pl.ds(own, small)]
            here.append(wires.send(piece, piece, place.along(second, apart)[1]))
        pending4.append(here)
    pending5, pending6 = [], []
    for p, (first, second, third, base, size) in enumerate(PARTS):
        block = size // AXIS[first]
        for copy in pending4[p]:
            copy.wait_recv()
        piece = full.at[pl.ds(k * HALF + base + at[first] * block, block)]
        pending5.append(
            [wires.send(piece, piece, place.along(first, apart)[1]) for apart in range(1, AXIS[first])]
        )
        pending6.append(wires.send(piece, piece, other))
    for p, (first, second, third, base, size) in enumerate(PARTS):
        block = size // AXIS[first]
        for apart in range(1, AXIS[first]):
            pending5[p][apart - 1].wait_recv()
            start = lax.rem(at[first] + AXIS[first] - apart, AXIS[first])
            piece = full.at[pl.ds(k * HALF + base + start * block, block)]
            pending6.append(wires.send(piece, piece, other))
    for copy in pending6:
        copy.wait_recv()


WIRES = 3 + 17 + 21 + 13 + 21 + 17 + 20


def scratch_of_reduce():
    tile = (8, 128)
    firsts = [pltpu.VMEM((AXIS[f], n // AXIS[f]) + tile, F32) for f, s, t, _, n in PARTS]
    small = [n // AXIS[f] // AXIS[s] for f, s, t, _, n in PARTS]
    seconds = [pltpu.VMEM((AXIS[p[1]], m) + tile, F32) for p, m in zip(PARTS, small)]
    thirds = [pltpu.VMEM((AXIS[p[2]], m) + tile, F32) for p, m in zip(PARTS, small)]
    sums1 = [pltpu.VMEM((n // AXIS[f],) + tile, F32) for f, s, t, _, n in PARTS]
    sums2 = [pltpu.VMEM((m,) + tile, F32) for m in small]
    return [
        pltpu.VMEM((2 * HALF,) + tile, F32),
        pltpu.VMEM((HALF,) + tile, F32),
        pltpu.VMEM((HALF,) + tile, F32),
        pltpu.VMEM((2 * HALF,) + tile, F32),
        firsts,
        seconds,
        thirds,
        sums1,
        sums2,
    ]


def greet(place, barrier, devices):
    for device in devices:
        pl.semaphore_signal(barrier, inc=1, device_id=device, device_id_type=MESH)


def tiles_in(local, enc, rel):
    for column in range(4):
        half, low = column // 2 * HALF, column % 2
        tiles = enc[:, column * 128 : column * 128 + 128].reshape(96, 8, 128)
        local[half + low * 96 : half + low * 96 + 96] = tiles
        tiles = rel[:, column * 128 : column * 128 + 128].reshape(2, 8, 128)
        local[half + 192 + low * 2 : half + 194 + low * 2] = tiles


def tiles_out(full, enc_ref, rel_ref):
    g = lax.axis_index("rel")
    for column in range(4):
        half, low = column // 2 * HALF, column % 2
        lanes = pl.ds(column * 128, 128)
        enc_ref[:, lanes] = full[half + low * 96 : half + low * 96 + 96].reshape(768, 128)
        rows = full[half + 192 + low * 2 : half + 194 + low * 2].reshape(16, 128)
        part = jnp.zeros((3, 128), F32)
        for group in range(4):
            part = jnp.where(g == group, rows[group * 3 : group * 3 + 3], part)
        rel_ref[:, lanes] = part


NT = (((1,), (1,)), ((), ()))
ROWS = 768
AUG = 320


def dot(a, b, dims=(((1,), (0,)), ((), ()))):
    return lax.dot_general(a, b, dims, preferred_element_type=F32)


def two_terms(value):
    high = value.astype(BF16)
    return high, (value - high.astype(F32)).astype(BF16)


def is_row(count, width, ids):
    return lax.broadcasted_iota(jnp.int32, (count, width), 0) == ids


def one_hot(count, width, ids):
    return jnp.where(is_row(count, width, ids), 1.0, 0.0).astype(BF16)


def gather_edges(edge_src, edge_tgt, hot, neg, label, shift, edges, shifts):
    edges[...] = jnp.zeros(edges.shape, jnp.int32)
    for pair, slots in enumerate(((0, 1), (3, 2))):
        for s, slot in enumerate(slots):
            row = slice(slot, slot + 1)
            which = hot[0, 0, slot, 1:2, :] + 2 * hot[0, 0, slot, 2:3, :]
            edges[pair, 4 * s : 4 * s + 1, 0:ROWS] = edge_src[0, 0, row, :]
            edges[pair, 4 * s + 1 : 4 * s + 2, 0:ROWS] = which
            edges[pair, 4 * s + 2 : 4 * s + 3, 0:ROWS] = edge_tgt[0, 0, row, :]
            edges[pair, 4 * s + 3 : 4 * s + 4, 0:ROWS] = label[0, 0, row, :]
            edges[pair, 4 * s : 4 * s + 1, ROWS : ROWS + NEG] = neg[0, 0, row, :]
    shifts[...] = jnp.concatenate([shift[...].astype(F32), jnp.zeros((13, EMB), F32)], 0).astype(BF16)


def meet_pair(e, s, g, z_half, source_t, block, tgt_sum, mixed):
    scale = EMB ** (-0.5)
    src_ids, which = e[4 * s : 4 * s + 1, :ROWS], e[4 * s + 1 : 4 * s + 2, :ROWS]
    tgt_ids, label = e[4 * s + 2 : 4 * s + 3, :ROWS], e[4 * s + 3 : 4 * s + 4, :ROWS]
    neg_ids = e[4 * s : 4 * s + 1, ROWS : ROWS + NEG]
    ends = jnp.concatenate([one_hot(256, ROWS, src_ids), one_hot(64, ROWS, which + 16 * g)], 0)
    query = dot(source_t[...], ends).astype(BF16)
    rows = slice(256 * s, 256 * s + 256)
    prob = 1.0 / (1.0 + jnp.exp(-scale * dot(block[rows], query)))
    times = jnp.sum(
        jnp.where(is_row(256, NEG, neg_ids - 256 * z_half), 1.0, 0.0), axis=1, keepdims=True
    )
    weight = times * (prob * (1.0 / NEG)).astype(BF16).astype(F32)
    weight = weight + jnp.where(
        is_row(256, ROWS, tgt_ids - 256 * z_half), prob - label.astype(F32), 0.0
    )
    high, low = two_terms(weight)
    tgt_sum[rows] += dot(high, query, NT) + dot(low, query, NT)
    mixed[:, rows] += dot(ends, high, NT) + dot(ends, low, NT)


class Group:
    def __init__(self, place, send_sems, recv_sems):
        self.place, self.send_sems, self.recv_sems, self.used, self.open = place, send_sems, recv_sems, 0, []
        self.k, self.z_half = place.at["k"], lax.div(place.at["z"], 4)

    def device(self, dx, dy, dz, k):
        at = self.place.at
        return self.place.device(
            x=lax.rem(at["x"] + 2 * dx, 4),
            y=at["y"] + dy * (1 - 2 * lax.rem(at["y"], 2)),
            z=lax.rem(at["z"] + 4 * dz, 8),
            k=k,
        )

    def peers(self):
        found = [
            self.device(dx, 0, dz, k) for dx in range(2) for dz in range(2) for k in range(2) if dx + dz
        ]
        return found + [self.place.other_core(), self.device(0, 1, 0, 0), self.device(0, 1, 0, 1)]

    def copy(self, src, dst, device, sem):
        made = pltpu.make_async_remote_copy(
            src_ref=src,
            dst_ref=dst,
            send_sem=self.send_sems.at[self.used],
            recv_sem=self.recv_sems.at[sem],
            device_id=device,
            device_id_type=MESH,
        )
        self.used += 1
        return made

    def send(self, src, dst, device, sem):
        made = self.copy(src, dst, device, sem)
        made.start()
        self.open.append((made, None))

    def send_if(self, when, src, dst, device, sem):
        made = self.copy(src, dst, device, sem)

        @pl.when(when)
        def _():
            made.start()

        self.open.append((made, when))

    def wait(self, dst, sem):
        pltpu.make_async_remote_copy(
            src_ref=dst,
            dst_ref=dst,
            send_sem=self.send_sems.at[0],
            recv_sem=self.recv_sems.at[sem],
            device_id=self.place.other_core(),
            device_id_type=MESH,
        ).wait_recv()

    def wait_if(self, when, dst, sem):
        @pl.when(when)
        def _():
            self.wait(dst, sem)

    def finish(self):
        for made, when in self.open:
            if when is None:
                made.wait_send()
            else:
                pl.when(when)(made.wait_send)


RECVS = 4 + 4 + 4 + 4 + 4 + 4
SENDS = 4 + 4 + 4 + 3 + 4 + 3


def meets(
    place, group, src_feat, tgt_feat, weight, shift, edge_src, edge_tgt, hot, neg, label, src_grad,
    tgt_grad, edges, shifts, edges_in, source, source_t, block, own_rows, act, feat_t, tgt_sum, mixed,
    src_part, src_in, tgt_in, greeted,
):
    k, z_half, q = group.k, group.z_half, lax.axis_index("rel")
    scale = EMB ** (-0.5)
    gather_edges(edge_src, edge_tgt, hot, neg, label, shift, edges, shifts)

    greeted()

    def to_consumers(kind, src_of, dst):
        for dx in range(2):
            for dz in range(2):
                args = (src_of(dx), dst, group.device(dx, 0, dz, dx), 4 * kind + 2 * dz + k)
                if dx + dz == 0:
                    group.send_if(k == 1, *args)
                else:
                    group.send(*args)

    shift_rows = pl.ds(256 + 16 * q, 16)
    to_consumers(0, lambda dx: edges.at[dx], edges_in.at[q])
    to_consumers(1, lambda dx: shifts, source.at[shift_rows])

    feats = jnp.concatenate([src_feat[...], tgt_feat[...]], 0)
    act[...] = jnp.tanh(dot(feats, weight[...]))
    own_rows[...] = act[...].astype(BF16)
    src_rows = pl.ds(64 * q, 64)
    to_consumers(2, lambda dx: own_rows.at[0:64], source.at[src_rows])
    for dy, there in ((0, 1 - k), (1, 0), (1, 1)):
        group.send(
            own_rows.at[64:192], block.at[pl.ds(256 * dy + 128 * k, 128)], group.device(0, dy, 0, there), 12 + 2 * dy + k
        )
    block[pl.ds(128 * k, 128)] = own_rows[64:192]

    @pl.when(k == 0)
    def _():
        edges_in[q] = edges[0]
        source[shift_rows] = shifts[...]
        source[src_rows] = own_rows[0:64]

    feat_t[...] = feats.astype(F32).T.astype(BF16)
    tgt_sum[...] = jnp.zeros(tgt_sum.shape, F32)
    mixed[...] = jnp.zeros(mixed.shape, F32)

    def from_producers(kind, dst_of):
        for dz in range(2):
            for there in range(2):
                theirs = lax.rem(z_half + dz, 2) * 2 + there
                args = (dst_of(theirs), 4 * kind + 2 * dz + there)
                if dz + there == 0:
                    group.wait_if(k == 1, *args)
                else:
                    group.wait(*args)

    from_producers(0, lambda g: edges_in.at[g])
    from_producers(1, lambda g: source.at[pl.ds(256 + 16 * g, 16)])
    from_producers(2, lambda g: source.at[pl.ds(64 * g, 64)])
    source_t[...] = source[...].astype(F32).T.astype(BF16)
    for dy, there in ((0, 1 - k), (1, 0), (1, 1)):
        group.wait(block.at[pl.ds(256 * dy + 128 * there, 128)], 12 + 2 * dy + there)

    @pl.loop(0, 4)
    def _(g):
        e = edges_in[g]
        for s in range(2):
            meet_pair(e, s, g, z_half, source_t, block, tgt_sum, mixed)

    high, low = two_terms(mixed[...])
    rows = block[...]
    src_part[...] = scale * (dot(high, rows) + dot(low, rows))
    for dz in range(2):
        for there in range(2):
            theirs = lax.rem(z_half + dz, 2) * 2 + there
            device = group.place.device(
                x=lax.rem(place.at["x"] + 2 * k, 4), z=lax.rem(place.at["z"] + 4 * dz, 8), k=there
            )
            args = (src_part.at[pl.ds(64 * theirs, 64)], src_in.at[2 * k + dz], device, 16 + 2 * k + dz)
            if dz + there == 0:
                group.send_if(k == 1, *args)
            else:
                group.send(*args)

    @pl.when(k == 0)
    def _():
        src_in[0] = src_part[pl.ds(64 * q, 64)]

    tgt_sum[...] = scale * tgt_sum[...]
    for dy, there in ((0, 1 - k), (1, 0), (1, 1)):
        group.send(
            tgt_sum.at[pl.ds(256 * dy + 128 * there, 128)], tgt_in.at[2 * dy + k], group.device(0, dy, 0, there), 20 + 2 * dy + k
        )
    group.wait_if(k == 1, src_in.at[0], 16)
    for slot in range(1, 4):
        group.wait(src_in.at[slot], 16 + slot)
    total = src_in[0] + src_in[1] + src_in[2] + src_in[3]
    src_grad[...] = total
    d_src = (total * (1.0 - act[0:64] * act[0:64])).astype(BF16)
    total = tgt_sum[pl.ds(128 * k, 128)]
    for dy, there in ((0, 1 - k), (1, 0), (1, 1)):
        group.wait(tgt_in.at[2 * dy + there], 20 + 2 * dy + there)
        total = total + tgt_in[2 * dy + there]
    tgt_grad[...] = total
    d_tgt = (total * (1.0 - act[64:192] * act[64:192])).astype(BF16)
    enc = dot(feat_t[...], jnp.concatenate([d_src, d_tgt], 0))
    rel = jnp.concatenate([src_part[256 + 16 * g : 259 + 16 * g] for g in range(4)] + [jnp.zeros((4, EMB), F32)], 0)
    return enc, rel


def scratch_of_meets():
    return [
        pltpu.VMEM((2, 8, 896), jnp.int32),
        pltpu.VMEM((16, EMB), BF16),
        pltpu.VMEM((4, 8, 896), jnp.int32),
        pltpu.VMEM((AUG, EMB), BF16),
        pltpu.VMEM((EMB, AUG), BF16),
        pltpu.VMEM((512, EMB), BF16),
        pltpu.VMEM((192, EMB), BF16),
        pltpu.VMEM((192, EMB), F32),
        pltpu.VMEM((768, 192), BF16),
        pltpu.VMEM((512, EMB), F32),
        pltpu.VMEM((AUG, 512), F32),
        pltpu.VMEM((AUG, EMB), F32),
        pltpu.VMEM((4, 64, EMB), F32),
        pltpu.VMEM((4, 128, EMB), F32),
    ]

def reduce_kernel(enc_ref, rel_ref, enc_out, rel_out, *scratch):
    *buffers, send_sems, recv_sems = scratch
    place = Place()
    barrier = pltpu.get_barrier_semaphore()
    others = [place.along(axis, apart)[1] for axis, n in AXIS.items() for apart in range(1, n)]
    others.append(place.other_core())
    greet(place, barrier, others)
    tiles_in(buffers[0], enc_ref[...], rel_ref[...])
    pl.semaphore_wait(barrier, len(others))
    wires = Wires(send_sems, recv_sems)
    reduce_everywhere(place, wires, *buffers)
    tiles_out(buffers[3], enc_out, rel_out)
    wires.finish()

def summed(enc, rel):
    return pl.pallas_call(
        reduce_kernel,
        out_shape=(jax.ShapeDtypeStruct((768, EMB), F32), jax.ShapeDtypeStruct((3, EMB), F32)),
        in_specs=[pl.BlockSpec(memory_space=pltpu.VMEM)] * 2,
        out_specs=(pl.BlockSpec(memory_space=pltpu.VMEM),) * 2,
        scratch_shapes=scratch_of_reduce()
        + [pltpu.SemaphoreType.DMA((WIRES,)), pltpu.SemaphoreType.DMA((WIRES,))],
        compiler_params=pltpu.CompilerParams(
            collective_id=0, has_side_effects=True, vmem_limit_bytes=40 * 2**20
        ),
    )(enc, rel)


def meet_kernel(*refs):
    inputs, (src_grad, tgt_grad, enc, rel), scratch = refs[:9], refs[9:13], refs[13:]
    *buffers, send_sems, recv_sems = scratch
    place = Place()
    group = Group(place, send_sems, recv_sems)
    barrier = pltpu.get_barrier_semaphore()
    others = group.peers()
    greet(place, barrier, others)
    enc[...], rel[...] = meets(
        place, group, *inputs, src_grad, tgt_grad, *buffers, lambda: pl.semaphore_wait(barrier, len(others))
    )
    group.finish()


def met(*arrays):
    shapes = ((64, EMB), (128, EMB), (768, EMB), (16, EMB))
    return pl.pallas_call(
        meet_kernel,
        out_shape=tuple(jax.ShapeDtypeStruct(shape, F32) for shape in shapes),
        in_specs=[pl.BlockSpec(memory_space=pltpu.VMEM)] * 9,
        out_specs=(pl.BlockSpec(memory_space=pltpu.VMEM),) * 4,
        scratch_shapes=scratch_of_meets()
        + [pltpu.SemaphoreType.DMA((SENDS,)), pltpu.SemaphoreType.DMA((RECVS,))],
        compiler_params=pltpu.CompilerParams(
            collective_id=1, has_side_effects=True, vmem_limit_bytes=48 * 2**20
        ),
    )(*arrays)


def shards(*arrays):
    src_grad, tgt_grad, enc, rel = met(*arrays)
    enc_grad, rel_grad = summed(enc, rel)
    return src_grad, tgt_grad, rel_grad, enc_grad


def solution(mesh):
    in_specs = (
        P(("bucket", "rel"), None),
        P(("bucket", "rel"), None),
        P(),
        P("rel", None),
        P("bucket", "rel", None, None),
        P("bucket", "rel", None, None),
        P("bucket", "rel", None, None, None),
        P("bucket", "rel", None, None),
        P("bucket", "rel", None, None),
    )
    out_specs = (P(("bucket", "rel"), None), P(("bucket", "rel"), None), P("rel", None), P())
    return jax.shard_map(shards, mesh=mesh, in_specs=in_specs, out_specs=out_specs, check_vma=False)
```

profile of v0, /device:TPU:1, one launch (start us, length us, event | category | flops | bytes accessed | tf_op | source)
XLA Modules:
  0.0 109.8 jit_solution(3748280959191005495)
XLA Ops:
  0.6 0.8 copy.13.refs_6_
  1.4 0.0 copy-start
  1.4 1.1 %copy-done = bf16[768,512]{1,0:T(8,128)(2,1)S(1)} copy-done((bf16[768,512]{1,0:T(8,128)(2,1)S(1)}, bf16[768,512]{1,0:T(8,128)(2,1)}, u32[]{:S(2)}) %copy-start) | copy-done | bytes 786456
  2.6 0.0 copy-start.1
  2.6 0.9 copy-done.1
  3.5 0.0 copy-start.2
  3.5 0.9 copy-done.2
  4.4 0.0 copy-start.3
  4.4 0.7 copy-done.3
  5.1 0.0 copy-start.4
  5.1 0.7 copy-done.4
  5.8 0.0 copy-start.5
  5.8 0.7 copy-done.5
  6.5 0.0 copy-start.6
  6.5 0.7 copy-done.6
  7.2 0.0 copy-start.7
  7.2 0.7 copy-done.7
  7.9 48.6 %shard_map.120 = (f32[64,512]{1,0:T(8,128)S(1)}, f32[128,512]{1,0:T(8,128)S(1)}, f32[768,512]{1,0:T(8,128)S(1)}, f32[16,512]{1,0:T(8,128)S(1)}) custom-call(bf16[64,768]{1,0:T(8,128)(2,1)S(1)} %copy-done.2, bf16[128,768]{1,0:T(8,128)(2,1)S(1)} %copy-done.1, bf16[768,512]{1,0:T(8,128)(2,1)S(1)} %copy-done, bf16[3,512]{1,0:T(4,128)(2,1)S(1)} %copy-done.6, ...), custom_call_target="tpu_custom_call" | custom-call | tf_op jit(solution)/shard_map/pallas_call | solution.py:506
  56.4 50.3 %shard_map.121 = (f32[768,512]{1,0:T(8,128)S(1)}, f32[3,512]{1,0:T(4,128)S(1)}) custom-call(f32[768,512]{1,0:T(8,128)S(1)} %get-tuple-element.12.enc_ref, f32[16,512]{1,0:T(8,128)S(1)} %get-tuple-element.13.rel_ref), custom_call_target="tpu_custom_call" | custom-call | tf_op jit(solution)/shard_map/pallas_call | solution.py:477
  106.7 0.7 copy.18
  107.4 0.7 copy.19
  108.1 0.6 copy.20
  108.7 1.1 %copy.21 = f32[768,512]{1,0:T(8,128)} copy(f32[768,512]{1,0:T(8,128)S(1)} %get-tuple-element.23) | data formatting | bytes 3145728
Async XLA Ops:
  1.4 1.1 %copy-start = (bf16[768,512]{1,0:T(8,128)(2,1)S(1)}, bf16[768,512]{1,0:T(8,128)(2,1)}, u32[]{:S(2)}) copy-start(bf16[768,512]{1,0:T(8,128)(2,1)} %refs_2_.1) | copy-start | bytes 2359300
  2.6 0.9 copy-start.1
  3.5 0.9 copy-start.2
  4.4 0.7 copy-start.3
  5.1 0.7 copy-start.4
  5.8 0.7 copy-start.5
  6.5 0.7 copy-start.6
  7.2 0.7 copy-start.7
where the time goes:
time: 110 us
  Pallas kernels  98.8 us (90%)
  local copies, waits for them, and re-layouts  10.3 us (9%)
    pallas_call x1, Pallas kernels, summed(): pl.pallas_call(reduce_kernel, out_shape=(jax.ShapeDtypeStruct((768, EMB),...  50.3 us
    pallas_call x1, Pallas kernels, met(): pl.pallas_call(meet_kernel, out_shape=tuple((jax.ShapeDtypeStruct(shape,...  48.6 us
    unnamed x21, local copies, waits for them, and re-layouts  10.3 us

commit v1 on v0

--- a/solution.py
+++ b/solution.py
@@ -16,6 +16,11 @@
 PARTS = (("z", "y", "x", 0, 64), ("y", "z", "x", 64, 64), ("x", "y", "z", 128, 96))
 
 
+def far_first(axis):
+    n = AXIS[axis]
+    return sorted(range(1, n), key=lambda apart: -min(apart, n - apart))
+
+
 class Place:
     def __init__(self):
         b, q = lax.axis_index("bucket"), lax.axis_index("rel")
@@ -62,15 +67,17 @@
             copy.wait_send()
 
 
-def reduce_everywhere(place, wires, local, pair, mine, full, firsts, seconds, thirds, sums1, sums2):
+def reduce_everywhere(place, wires, local, pair, mine, full, firsts, seconds, thirds, sums1, sums2, fill):
     at, k = place.at, place.at["k"]
     other = place.other_core()
     copies = []
+    fill(1 - k)
     for _, _, _, base, size in PARTS:
         size = min(size, 196 - base)
         copies.append(
             wires.send(local.at[pl.ds((1 - k) * HALF + base, size)], pair.at[pl.ds(base, size)], other)
         )
+    fill(k)
     mine[pl.ds(196, 28)] = jnp.zeros((28, 8, 128), F32)
     pending1 = []
     for p, (first, _, _, base, size) in enumerate(PARTS):
@@ -78,46 +85,42 @@
         real = min(size, 196 - base)
         mine[pl.ds(base, real)] = local[pl.ds(k * HALF + base, real)] + pair[pl.ds(base, real)]
         block = size // AXIS[first]
-        here = []
-        for apart in range(1, AXIS[first]):
+        here = {}
+        for apart in far_first(first):
             there, device = place.along(first, apart)
-            here.append(
-                wires.send(mine.at[pl.ds(base + there * block, block)], firsts[p].at[apart], device)
-            )
+            here[apart] = wires.send(mine.at[pl.ds(base + there * block, block)], firsts[p].at[apart], device)
         pending1.append(here)
     pending2 = []
     for p, (first, second, _, base, size) in enumerate(PARTS):
         block = size // AXIS[first]
         total = mine[pl.ds(base + at[first] * block, block)]
         for apart in range(1, AXIS[first]):
-            pending1[p][apart - 1].wait_recv()
+            pending1[p][apart].wait_recv()
             total = total + firsts[p][apart]
         sums1[p][...] = total
         small = block // AXIS[second]
-        here = []
-        for apart in range(1, AXIS[second]):
+        here = {}
+        for apart in far_first(second):
             there, device = place.along(second, apart)
-            here.append(
-                wires.send(sums1[p].at[pl.ds(there * small, small)], seconds[p].at[apart], device)
-            )
+            here[apart] = wires.send(sums1[p].at[pl.ds(there * small, small)], seconds[p].at[apart], device)
         pending2.append(here)
     pending3 = []
     for p, (first, second, third, base, size) in enumerate(PARTS):
         small = size // AXIS[first] // AXIS[second]
         total = sums1[p][pl.ds(at[second] * small, small)]
         for apart in range(1, AXIS[second]):
-            pending2[p][apart - 1].wait_recv()
+            pending2[p][apart].wait_recv()
             total = total + seconds[p][apart]
         sums2[p][...] = total
-        here = []
-        for apart in range(1, AXIS[third]):
-            here.append(wires.send(sums2[p], thirds[p].at[apart], place.along(third, apart)[1]))
+        here = {}
+        for apart in far_first(third):
+            here[apart] = wires.send(sums2[p], thirds[p].at[apart], place.along(third, apart)[1])
         pending3.append(here)
     pending4 = []
     for p, (first, second, third, base, size) in enumerate(PARTS):
         thirds[p][0] = sums2[p][...]
         for apart in range(1, AXIS[third]):
-            pending3[p][apart - 1].wait_recv()
+            pending3[p][apart].wait_recv()
         total = 0.0
         for where in range(AXIS[third]):
             total = total + thirds[p][lax.rem(at[third] + AXIS[third] - where, AXIS[third])]
@@ -126,7 +129,7 @@
         own = k * HALF + base + at[first] * block + at[second] * small
         full[pl.ds(own, small)] = total
         here = []
-        for apart in range(1, AXIS[second]):
+        for apart in far_first(second):
             piece = full.at[pl.ds(own, small)]
             here.append(wires.send(piece, piece, place.along(second, apart)[1]))
         pending4.append(here)
@@ -137,13 +140,13 @@
             copy.wait_recv()
         piece = full.at[pl.ds(k * HALF + base + at[first] * block, block)]
         pending5.append(
-            [wires.send(piece, piece, place.along(first, apart)[1]) for apart in range(1, AXIS[first])]
+            {apart: wires.send(piece, piece, place.along(first, apart)[1]) for apart in far_first(first)}
         )
         pending6.append(wires.send(piece, piece, other))
     for p, (first, second, third, base, size) in enumerate(PARTS):
         block = size // AXIS[first]
-        for apart in range(1, AXIS[first]):
-            pending5[p][apart - 1].wait_recv()
+        for apart in reversed(far_first(first)):
+            pending5[p][apart].wait_recv()
             start = lax.rem(at[first] + AXIS[first] - apart, AXIS[first])
             piece = full.at[pl.ds(k * HALF + base + start * block, block)]
             pending6.append(wires.send(piece, piece, other))
@@ -180,15 +183,6 @@
         pl.semaphore_signal(barrier, inc=1, device_id=device, device_id_type=MESH)
 
 
-def tiles_in(local, enc, rel):
-    for column in range(4):
-        half, low = column // 2 * HALF, column % 2
-        tiles = enc[:, column * 128 : column * 128 + 128].reshape(96, 8, 128)
-        local[half + low * 96 : half + low * 96 + 96] = tiles
-        tiles = rel[:, column * 128 : column * 128 + 128].reshape(2, 8, 128)
-        local[half + 192 + low * 2 : half + 194 + low * 2] = tiles
-
-
 def tiles_out(full, enc_ref, rel_ref):
     g = lax.axis_index("rel")
     for column in range(4):
@@ -225,24 +219,37 @@
 
 
 def gather_edges(edge_src, edge_tgt, hot, neg, label, shift, edges, shifts):
-    edges[...] = jnp.zeros(edges.shape, jnp.int32)
+    edges[...] = jnp.zeros(edges.shape, jnp.int16)
     for pair, slots in enumerate(((0, 1), (3, 2))):
         for s, slot in enumerate(slots):
             row = slice(slot, slot + 1)
-            which = hot[0, 0, slot, 1:2, :] + 2 * hot[0, 0, slot, 2:3, :]
-            edges[pair, 4 * s : 4 * s + 1, 0:ROWS] = edge_src[0, 0, row, :]
-            edges[pair, 4 * s + 1 : 4 * s + 2, 0:ROWS] = which
-            edges[pair, 4 * s + 2 : 4 * s + 3, 0:ROWS] = edge_tgt[0, 0, row, :]
-            edges[pair, 4 * s + 3 : 4 * s + 4, 0:ROWS] = label[0, 0, row, :]
-            edges[pair, 4 * s : 4 * s + 1, ROWS : ROWS + NEG] = neg[0, 0, row, :]
-    shifts[...] = jnp.concatenate([shift[...].astype(F32), jnp.zeros((13, EMB), F32)], 0).astype(BF16)
+            whole = [
+                edge_src[0, 0, row, :],
+                edge_tgt[0, 0, row, :],
+                label[0, 0, row, :],
+                hot[0, 0, 1, row, :],
+                hot[0, 0, 2, row, :],
+            ]
+            rows = [part[:, h : h + ROWS // 2] for part in whole for h in (0, ROWS // 2)]
+            rows.append(jnp.concatenate([neg[0, 0, row, :], jnp.zeros((1, ROWS // 2 - NEG), jnp.int32)], 1))
+            rows.append(jnp.zeros((5, ROWS // 2), jnp.int32))
+            edges[pair, 16 * s : 16 * s + 16] = jnp.concatenate(rows, 0).astype(jnp.int16)
+    parts = [shift[:, c : c + 128].astype(F32) for c in range(0, EMB, 128)]
+    shifts[...] = jnp.concatenate(parts + [jnp.zeros((4, 128), F32)], 0).astype(BF16)
+
+
+def spread_shifts(shifts, source):
+    for g in range(4):
+        got = shifts[g].astype(F32)
+        rows = jnp.concatenate([got[3 * c : 3 * c + 3] for c in range(4)], 1)
+        source[256 + 16 * g : 272 + 16 * g] = jnp.concatenate([rows, jnp.zeros((13, EMB), F32)], 0).astype(BF16)
 
 
 def meet_pair(e, s, g, z_half, source_t, block, tgt_sum, mixed):
     scale = EMB ** (-0.5)
-    src_ids, which = e[4 * s : 4 * s + 1, :ROWS], e[4 * s + 1 : 4 * s + 2, :ROWS]
-    tgt_ids, label = e[4 * s + 2 : 4 * s + 3, :ROWS], e[4 * s + 3 : 4 * s + 4, :ROWS]
-    neg_ids = e[4 * s : 4 * s + 1, ROWS : ROWS + NEG]
+    rows = [jnp.concatenate([e[i : i + 1], e[i + 1 : i + 2]], 1) for i in range(0, 10, 2)]
+    src_ids, tgt_ids, label, which = rows[0], rows[1], rows[2], rows[3] + 2 * rows[4]
+    neg_ids = e[10:11, :NEG]
     ends = jnp.concatenate([one_hot(256, ROWS, src_ids), one_hot(64, ROWS, which + 16 * g)], 0)
     query = dot(source_t[...], ends).astype(BF16)
     rows = slice(256 * s, 256 * s + 256)
@@ -274,10 +281,8 @@
         )
 
     def peers(self):
-        found = [
-            self.device(dx, 0, dz, k) for dx in range(2) for dz in range(2) for k in range(2) if dx + dz
-        ]
-        return found + [self.place.other_core(), self.device(0, 1, 0, 0), self.device(0, 1, 0, 1)]
+        found = [self.device(dx, 0, dz, 1 - self.k) for dx, dz in ((0, 1), (1, 0), (1, 1))]
+        return found + [self.device(1, 0, 1, self.k), self.device(0, 1, 0, 1 - self.k)]
 
     def copy(self, src, dst, device, sem):
         made = pltpu.make_async_remote_copy(
@@ -333,35 +338,37 @@
 
 
 def meets(
-    place, group, src_feat, tgt_feat, weight, shift, edge_src, edge_tgt, hot, neg, label, src_grad,
-    tgt_grad, edges, shifts, edges_in, source, source_t, block, own_rows, act, feat_t, tgt_sum, mixed,
-    src_part, src_in, tgt_in, greeted,
+    place, group, fetched, edges, shifts, edges_in, shifts_in, source, source_t, block, own_rows, act,
+    feat_t, tgt_sum, mixed, src_part, src_in, tgt_in, grads, src_grad, tgt_grad, greeted,
 ):
     k, z_half, q = group.k, group.z_half, lax.axis_index("rel")
     scale = EMB ** (-0.5)
-    gather_edges(edge_src, edge_tgt, hot, neg, label, shift, edges, shifts)
+    src_feat, tgt_feat, weight, shift, edge_src, edge_tgt, hot, neg, label = fetched
+    for ref in (edge_src, edge_tgt, hot, neg, label, shift):
+        ref.wait()
+    gather_edges(*(ref.here for ref in (edge_src, edge_tgt, hot, neg, label, shift)), edges, shifts)
+    for ref in (src_feat, tgt_feat, weight):
+        ref.wait()
+    feats = jnp.concatenate([src_feat.here[...], tgt_feat.here[...]], 0)
+    act[...] = jnp.tanh(dot(feats, weight.here[...]))
+    own_rows[...] = act[...].astype(BF16)
 
     greeted()
 
     def to_consumers(kind, src_of, dst):
         for dx in range(2):
-            for dz in range(2):
+            for dz in (1, 0):
                 args = (src_of(dx), dst, group.device(dx, 0, dz, dx), 4 * kind + 2 * dz + k)
                 if dx + dz == 0:
                     group.send_if(k == 1, *args)
                 else:
                     group.send(*args)
 
-    shift_rows = pl.ds(256 + 16 * q, 16)
-    to_consumers(0, lambda dx: edges.at[dx], edges_in.at[q])
-    to_consumers(1, lambda dx: shifts, source.at[shift_rows])
-
-    feats = jnp.concatenate([src_feat[...], tgt_feat[...]], 0)
-    act[...] = jnp.tanh(dot(feats, weight[...]))
-    own_rows[...] = act[...].astype(BF16)
     src_rows = pl.ds(64 * q, 64)
     to_consumers(2, lambda dx: own_rows.at[0:64], source.at[src_rows])
-    for dy, there in ((0, 1 - k), (1, 0), (1, 1)):
+    to_consumers(0, lambda dx: edges.at[dx], edges_in.at[q])
+    to_consumers(1, lambda dx: shifts, shifts_in.at[q])
+    for dy, there in ((1, 0), (1, 1), (0, 1 - k)):
         group.send(
             own_rows.at[64:192], block.at[pl.ds(256 * dy + 128 * k, 128)], group.device(0, dy, 0, there), 12 + 2 * dy + k
         )
@@ -370,7 +377,7 @@
     @pl.when(k == 0)
     def _():
         edges_in[q] = edges[0]
-        source[shift_rows] = shifts[...]
+        shifts_in[q] = shifts[...]
         source[src_rows] = own_rows[0:64]
 
     feat_t[...] = feats.astype(F32).T.astype(BF16)
@@ -388,22 +395,36 @@
                     group.wait(*args)
 
     from_producers(0, lambda g: edges_in.at[g])
-    from_producers(1, lambda g: source.at[pl.ds(256 + 16 * g, 16)])
+    from_producers(1, lambda g: shifts_in.at[g])
+    spread_shifts(shifts_in, source)
     from_producers(2, lambda g: source.at[pl.ds(64 * g, 64)])
     source_t[...] = source[...].astype(F32).T.astype(BF16)
     for dy, there in ((0, 1 - k), (1, 0), (1, 1)):
         group.wait(block.at[pl.ds(256 * dy + 128 * there, 128)], 12 + 2 * dy + there)
 
-    @pl.loop(0, 4)
-    def _(g):
-        e = edges_in[g]
-        for s in range(2):
-            meet_pair(e, s, g, z_half, source_t, block, tgt_sum, mixed)
+    def send_tgt(dy, there):
+        rows = pl.ds(256 * dy + 128 * there, 128)
+        tgt_sum[rows] = scale * tgt_sum[rows]
+        group.send(
+            tgt_sum.at[rows], tgt_in.at[2 * dy + k], group.device(0, dy, 0, there), 20 + 2 * dy + k
+        )
+
+    for s in (1, 0):
+
+        @pl.loop(0, 2)
+        def _(turn):
+            for g in range(2):
+                e = edges_in[2 * turn + g, 16 * s : 16 * s + 16].astype(jnp.int32)
+                meet_pair(e, s, 2 * turn + g, z_half, source_t, block, tgt_sum, mixed)
+
+        if s == 1:
+            send_tgt(1, 0)
+            send_tgt(1, 1)
 
     high, low = two_terms(mixed[...])
     rows = block[...]
     src_part[...] = scale * (dot(high, rows) + dot(low, rows))
-    for dz in range(2):
+    for dz in (1, 0):
         for there in range(2):
             theirs = lax.rem(z_half + dz, 2) * 2 + there
             device = group.place.device(
@@ -419,33 +440,38 @@
     def _():
         src_in[0] = src_part[pl.ds(64 * q, 64)]
 
-    tgt_sum[...] = scale * tgt_sum[...]
+    send_tgt(0, 1 - k)
+    total = scale * tgt_sum[pl.ds(128 * k, 128)]
     for dy, there in ((0, 1 - k), (1, 0), (1, 1)):
-        group.send(
-            tgt_sum.at[pl.ds(256 * dy + 128 * there, 128)], tgt_in.at[2 * dy + k], group.device(0, dy, 0, there), 20 + 2 * dy + k
-        )
+        group.wait(tgt_in.at[2 * dy + there], 20 + 2 * dy + there)
+        total = total + tgt_in[2 * dy + there]
+    tgt_grad[...] = total
+    grads[64:192] = (total * (1.0 - act[64:192] * act[64:192])).astype(BF16)
     group.wait_if(k == 1, src_in.at[0], 16)
     for slot in range(1, 4):
         group.wait(src_in.at[slot], 16 + slot)
     total = src_in[0] + src_in[1] + src_in[2] + src_in[3]
     src_grad[...] = total
-    d_src = (total * (1.0 - act[0:64] * act[0:64])).astype(BF16)
-    total = tgt_sum[pl.ds(128 * k, 128)]
-    for dy, there in ((0, 1 - k), (1, 0), (1, 1)):
-        group.wait(tgt_in.at[2 * dy + there], 20 + 2 * dy + there)
-        total = total + tgt_in[2 * dy + there]
-    tgt_grad[...] = total
-    d_tgt = (total * (1.0 - act[64:192] * act[64:192])).astype(BF16)
-    enc = dot(feat_t[...], jnp.concatenate([d_src, d_tgt], 0))
-    rel = jnp.concatenate([src_part[256 + 16 * g : 259 + 16 * g] for g in range(4)] + [jnp.zeros((4, EMB), F32)], 0)
-    return enc, rel
+    grads[0:64] = (total * (1.0 - act[0:64] * act[0:64])).astype(BF16)
+
+
+def local_sums(half, local, feat_t, grads, src_part):
+    lanes = pl.ds(pl.multiple_of(256 * half, 256), 256)
+    enc = dot(feat_t[...], grads[:, lanes])
+    rel = [src_part[256 + 16 * g : 259 + 16 * g, lanes] for g in range(4)]
+    rel = jnp.concatenate(rel + [jnp.zeros((4, 256), F32)], 0)
+    for low in range(2):
+        cut = slice(128 * low, 128 * low + 128)
+        local[pl.ds(half * HALF + low * 96, 96)] = enc[:, cut].reshape(96, 8, 128)
+        local[pl.ds(half * HALF + 192 + low * 2, 2)] = rel[:, cut].reshape(2, 8, 128)
 
 
 def scratch_of_meets():
     return [
-        pltpu.VMEM((2, 8, 896), jnp.int32),
-        pltpu.VMEM((16, EMB), BF16),
-        pltpu.VMEM((4, 8, 896), jnp.int32),
+        pltpu.VMEM((2, 32, 384), jnp.int16),
+        pltpu.VMEM((16, 128), BF16),
+        pltpu.VMEM((4, 32, 384), jnp.int16),
+        pltpu.VMEM((4, 16, 128), BF16),
         pltpu.VMEM((AUG, EMB), BF16),
         pltpu.VMEM((EMB, AUG), BF16),
         pltpu.VMEM((512, EMB), BF16),
@@ -457,68 +483,92 @@
         pltpu.VMEM((AUG, EMB), F32),
         pltpu.VMEM((4, 64, EMB), F32),
         pltpu.VMEM((4, 128, EMB), F32),
+        pltpu.VMEM((192, EMB), BF16),
     ]
 
-def reduce_kernel(enc_ref, rel_ref, enc_out, rel_out, *scratch):
-    *buffers, send_sems, recv_sems = scratch
+
+class Fetched:
+    def __init__(self, there, here, sem):
+        self.here, self.copy = here, pltpu.make_async_copy(there, here, sem)
+        self.copy.start()
+
+    def wait(self):
+        self.copy.wait()
+
+
+def kernel(*refs):
+    inputs, outputs, (here, meet_buffers, sum_buffers, fetch_sems, *sems) = refs[:9], refs[9:13], refs[13:]
+    src_grad, tgt_grad, enc_grad, rel_grad = outputs
     place = Place()
+    group = Group(place, sems[0], sems[1])
     barrier = pltpu.get_barrier_semaphore()
     others = [place.along(axis, apart)[1] for axis, n in AXIS.items() for apart in range(1, n)]
-    others.append(place.other_core())
+    others += [place.other_core()] + group.peers()
+    fetched = [None] * 9
+    for i in (4, 5, 6, 7, 8, 3, 0, 1, 2):
+        fetched[i] = Fetched(inputs[i], here[i], fetch_sems.at[i])
     greet(place, barrier, others)
-    tiles_in(buffers[0], enc_ref[...], rel_ref[...])
-    pl.semaphore_wait(barrier, len(others))
-    wires = Wires(send_sems, recv_sems)
-    reduce_everywhere(place, wires, *buffers)
-    tiles_out(buffers[3], enc_out, rel_out)
+    meets(
+        place, group, fetched, *meet_buffers, src_grad, tgt_grad, lambda: pl.semaphore_wait(barrier, len(others))
+    )
+    feat_t, src_part, grads = meet_buffers[9], meet_buffers[12], meet_buffers[15]
+    wires = Wires(sems[2], sems[3])
+    reduce_everywhere(
+        place, wires, *sum_buffers, lambda half: local_sums(half, sum_buffers[0], feat_t, grads, src_part)
+    )
+    tiles_out(sum_buffers[3], enc_grad, rel_grad)
+    group.finish()
     wires.finish()
 
-def summed(enc, rel):
-    return pl.pallas_call(
-        reduce_kernel,
-        out_shape=(jax.ShapeDtypeStruct((768, EMB), F32), jax.ShapeDtypeStruct((3, EMB), F32)),
-        in_specs=[pl.BlockSpec(memory_space=pltpu.VMEM)] * 2,
-        out_specs=(pl.BlockSpec(memory_space=pltpu.VMEM),) * 2,
-        scratch_shapes=scratch_of_reduce()
-        + [pltpu.SemaphoreType.DMA((WIRES,)), pltpu.SemaphoreType.DMA((WIRES,))],
+
+def hand_over(*refs):
+    results, outputs, rooms, in_sems, out_sems = refs[:4], refs[4:8], *refs[8:]
+    loads = [pltpu.make_async_copy(results[i], rooms[i], in_sems.at[i]) for i in range(4)]
+    stores = [pltpu.make_async_copy(rooms[i], outputs[i], out_sems.at[i]) for i in range(4)]
+    for load in loads:
+        load.start()
+    for load, store in zip(loads, stores):
+        load.wait()
+        store.start()
+    for store in stores:
+        store.wait()
+
+
+def shards(*arrays):
+    hot = jnp.transpose(arrays[6], (0, 1, 3, 2, 4))
+    arrays = arrays[:6] + (hot,) + arrays[7:]
+    shapes = ((64, EMB), (128, EMB), (768, EMB), (3, EMB))
+    results = pl.pallas_call(
+        kernel,
+        out_shape=tuple(jax.ShapeDtypeStruct(shape, F32) for shape in shapes),
+        in_specs=[pl.BlockSpec(memory_space=pl.ANY)] * 9,
+        out_specs=(pl.BlockSpec(memory_space=pltpu.VMEM),) * 4,
+        scratch_shapes=[
+            [pltpu.VMEM(array.shape, array.dtype) for array in arrays],
+            scratch_of_meets(),
+            scratch_of_reduce(),
+            pltpu.SemaphoreType.DMA((9,)),
+            pltpu.SemaphoreType.DMA((SENDS,)),
+            pltpu.SemaphoreType.DMA((RECVS,)),
+            pltpu.SemaphoreType.DMA((WIRES,)),
+            pltpu.SemaphoreType.DMA((WIRES,)),
+        ],
         compiler_params=pltpu.CompilerParams(
-            collective_id=0, has_side_effects=True, vmem_limit_bytes=40 * 2**20
-        ),
-    )(enc, rel)
-
-
-def meet_kernel(*refs):
-    inputs, (src_grad, tgt_grad, enc, rel), scratch = refs[:9], refs[9:13], refs[13:]
-    *buffers, send_sems, recv_sems = scratch
-    place = Place()
-    group = Group(place, send_sems, recv_sems)
-    barrier = pltpu.get_barrier_semaphore()
-    others = group.peers()
-    greet(place, barrier, others)
-    enc[...], rel[...] = meets(
-        place, group, *inputs, src_grad, tgt_grad, *buffers, lambda: pl.semaphore_wait(barrier, len(others))
-    )
-    group.finish()
-
-
-def met(*arrays):
-    shapes = ((64, EMB), (128, EMB), (768, EMB), (16, EMB))
-    return pl.pallas_call(
-        meet_kernel,
-        out_shape=tuple(jax.ShapeDtypeStruct(shape, F32) for shape in shapes),
-        in_specs=[pl.BlockSpec(memory_space=pltpu.VMEM)] * 9,
-        out_specs=(pl.BlockSpec(memory_space=pltpu.VMEM),) * 4,
-        scratch_shapes=scratch_of_meets()
-        + [pltpu.SemaphoreType.DMA((SENDS,)), pltpu.SemaphoreType.DMA((RECVS,))],
-        compiler_params=pltpu.CompilerParams(
-            collective_id=1, has_side_effects=True, vmem_limit_bytes=48 * 2**20
+            collective_id=0, has_side_effects=True, vmem_limit_bytes=56 * 2**20
         ),
     )(*arrays)
-
-
-def shards(*arrays):
-    src_grad, tgt_grad, enc, rel = met(*arrays)
-    enc_grad, rel_grad = summed(enc, rel)
+    src_grad, tgt_grad, enc_grad, rel_grad = pl.pallas_call(
+        hand_over,
+        out_shape=tuple(jax.ShapeDtypeStruct(shape, F32) for shape in shapes),
+        in_specs=[pl.BlockSpec(memory_space=pl.ANY)] * 4,
+        out_specs=(pl.BlockSpec(memory_space=pl.ANY),) * 4,
+        scratch_shapes=[
+            [pltpu.VMEM(shape, F32) for shape in shapes],
+            pltpu.SemaphoreType.DMA((4,)),
+            pltpu.SemaphoreType.DMA((4,)),
+        ],
+        compiler_params=pltpu.CompilerParams(vmem_limit_bytes=56 * 2**20),
+    )(*results)
     return src_grad, tgt_grad, rel_grad, enc_grad
 
 

time: 110 us -> 97.2 us (0.88)
  local copies, waits for them, and re-layouts: 10.3 us -> 0 us
  Pallas kernels: 98.8 us -> 96.4 us
    unnamed x21 -> x0, local copies, waits for them, and re-layouts: 10.3 us -> none
    pallas_call x2, Pallas kernels: 98.8 us -> 96.4 us  [the longest x1 93.6 us: shards(): pl.pallas_call(kernel, out_shape=tuple((jax.ShapeDtypeStruct(shape, F32)...]
where the time goes in v1:
time: 97.2 us; the launch traced here: 97 us
  Pallas kernels  96.4 us (99%)
    pallas_call x1, Pallas kernels, shards(): pl.pallas_call(kernel, out_shape=tuple((jax.ShapeDtypeStruct(shape, F32)...  93.6 us
    pallas_call x1, Pallas kernels, shards(): pl.pallas_call(hand_over, out_shape=tuple((jax.ShapeDtypeStruct(shape, F3...  2.78 us

profile of v1, /device:TPU:1, one launch (start us, length us, event | category | flops | bytes accessed | tf_op | source)
XLA Modules:
  0.0 97.0 jit_solution(55732453977186367)
XLA Ops:
  0.6 93.6 %shard_map.120 = (f32[64,512]{1,0:T(8,128)}, f32[128,512]{1,0:T(8,128)}, f32[768,512]{1,0:T(8,128)}, f32[3,512]{1,0:T(4,128)}) custom-call(bf16[64,768]{1,0:T(8,128)(2,1)} %refs_0_.1, bf16[128,768]{1,0:T(8,128)(2,1)} %refs_1_.1, bf16[768,512]{1,0:T(8,128)(2,1)} %refs_2_.1, bf16[3,512]{1,0:T(4,128)(2,1)} %refs_3_.1, s32[1,1,4,768]{3,2,1,0:T(4,128)} %refs_4_.1, ...), custom_call_target="tpu_custom_call" | custom-call | tf_op jit(solution)/shard_map/pallas_call | solution.py:541
  94.3 2.8 %shard_map.121 = (f32[64,512]{1,0:T(8,128)}, f32[128,512]{1,0:T(8,128)}, f32[768,512]{1,0:T(8,128)}, f32[3,512]{1,0:T(4,128)}) custom-call(f32[64,512]{1,0:T(8,128)} %get-tuple-element.12.refs_0_, f32[128,512]{1,0:T(8,128)} %get-tuple-element.13.refs_1_, f32[768,512]{1,0:T(8,128)} %get-tuple-element.14.refs_2_, f32[3,512]{1,0:T(4,128)} %get-tuple-element.15.refs_3_), custom_call_target="tpu_custom_call" | custom-call | tf_op jit(solution)/shard_map/pallas_call | solution.py:560

commit v2 on v1

--- a/solution.py
+++ b/solution.py
@@ -266,6 +266,19 @@
     mixed[:, rows] += dot(ends, high, NT) + dot(ends, low, NT)
 
 
+def narrowed(value):
+    most = jnp.maximum(jnp.max(jnp.abs(value), axis=0, keepdims=True), 1e-30)
+    whole = jnp.floor(value * (32767.0 / most) + 0.5).astype(jnp.int32).astype(jnp.int16)
+    step = most * (1.0 / 32767.0)
+    rows = [step[:, c : c + 128] for c in range(0, EMB, 128)]
+    return whole, jnp.concatenate(rows + [jnp.zeros((4, 128), F32)], 0)
+
+
+def widened(whole, steps):
+    step = jnp.concatenate([steps[c : c + 1] for c in range(4)], 1)
+    return whole.astype(jnp.int32).astype(F32) * step
+
+
 class Group:
     def __init__(self, place, send_sems, recv_sems):
         self.place, self.send_sems, self.recv_sems, self.used, self.open = place, send_sems, recv_sems, 0, []
@@ -333,13 +346,14 @@
                 pl.when(when)(made.wait_send)
 
 
-RECVS = 4 + 4 + 4 + 4 + 4 + 4
-SENDS = 4 + 4 + 4 + 3 + 4 + 3
+RECVS = 4 + 4 + 4 + 4 + 4 + 4 + 4
+SENDS = 4 + 4 + 4 + 3 + 8 + 3
 
 
 def meets(
     place, group, fetched, edges, shifts, edges_in, shifts_in, source, source_t, block, own_rows, act,
-    feat_t, tgt_sum, mixed, src_part, src_in, tgt_in, grads, src_grad, tgt_grad, greeted,
+    feat_t, tgt_sum, mixed, src_part, src_in, tgt_in, grads, src_out, steps_out,
+    steps_in, src_grad, tgt_grad, greeted,
 ):
     k, z_half, q = group.k, group.z_half, lax.axis_index("rel")
     scale = EMB ** (-0.5)
@@ -424,21 +438,30 @@
     high, low = two_terms(mixed[...])
     rows = block[...]
     src_part[...] = scale * (dot(high, rows) + dot(low, rows))
+    for part in range(4):
+        rows = slice(64 * part, 64 * part + 64)
+        src_out[rows], steps_out[part] = narrowed(src_part[rows])
     for dz in (1, 0):
         for there in range(2):
             theirs = lax.rem(z_half + dz, 2) * 2 + there
             device = group.place.device(
                 x=lax.rem(place.at["x"] + 2 * k, 4), z=lax.rem(place.at["z"] + 4 * dz, 8), k=there
             )
-            args = (src_part.at[pl.ds(64 * theirs, 64)], src_in.at[2 * k + dz], device, 16 + 2 * k + dz)
-            if dz + there == 0:
-                group.send_if(k == 1, *args)
-            else:
-                group.send(*args)
+            slot = 2 * k + dz
+            both = (
+                (src_out.at[pl.ds(64 * theirs, 64)], src_in.at[slot], device, 16 + slot),
+                (steps_out.at[theirs], steps_in.at[slot], device, 24 + slot),
+            )
+            for args in both:
+                if dz + there == 0:
+                    group.send_if(k == 1, *args)
+                else:
+                    group.send(*args)
 
     @pl.when(k == 0)
     def _():
-        src_in[0] = src_part[pl.ds(64 * q, 64)]
+        src_in[0] = src_out[pl.ds(64 * q, 64)]
+        steps_in[0] = steps_out[q]
 
     send_tgt(0, 1 - k)
     total = scale * tgt_sum[pl.ds(128 * k, 128)]
@@ -448,9 +471,12 @@
     tgt_grad[...] = total
     grads[64:192] = (total * (1.0 - act[64:192] * act[64:192])).astype(BF16)
     group.wait_if(k == 1, src_in.at[0], 16)
+    group.wait_if(k == 1, steps_in.at[0], 24)
+    total = widened(src_in[0], steps_in[0])
     for slot in range(1, 4):
         group.wait(src_in.at[slot], 16 + slot)
-    total = src_in[0] + src_in[1] + src_in[2] + src_in[3]
+        group.wait(steps_in.at[slot], 24 + slot)
+        total = total + widened(src_in[slot], steps_in[slot])
     src_grad[...] = total
     grads[0:64] = (total * (1.0 - act[0:64] * act[0:64])).astype(BF16)
 
@@ -481,9 +507,12 @@
         pltpu.VMEM((512, EMB), F32),
         pltpu.VMEM((AUG, 512), F32),
         pltpu.VMEM((AUG, EMB), F32),
-        pltpu.VMEM((4, 64, EMB), F32),
+        pltpu.VMEM((4, 64, EMB), jnp.int16),
         pltpu.VMEM((4, 128, EMB), F32),
         pltpu.VMEM((192, EMB), BF16),
+        pltpu.VMEM((256, EMB), jnp.int16),
+        pltpu.VMEM((4, 8, 128), F32),
+        pltpu.VMEM((4, 8, 128), F32),
     ]
 
 

time: 97.2 us -> 92.6 us (0.953)
  Pallas kernels: 96.4 us -> 91.8 us
    pallas_call x1, Pallas kernels: 93.6 us -> 89 us  [shards(): pl.pallas_call(kernel, out_shape=tuple((jax.ShapeDtypeStruct(shape, F32)...]
where the time goes in v2:
time: 92.6 us; the launch traced here: 92.5 us
  Pallas kernels  91.8 us (99%)
    pallas_call x1, Pallas kernels, shards(): pl.pallas_call(kernel, out_shape=tuple((jax.ShapeDtypeStruct(shape, F32)...  89 us
    pallas_call x1, Pallas kernels, shards(): pl.pallas_call(hand_over, out_shape=tuple((jax.ShapeDtypeStruct(shape, F3...  2.78 us

profile of v2, /device:TPU:1, one launch (start us, length us, event | category | flops | bytes accessed | tf_op | source)
XLA Modules:
  0.0 92.5 jit_solution(3221198379738374242)
XLA Ops:
  0.6 89.0 %shard_map.120 = (f32[64,512]{1,0:T(8,128)}, f32[128,512]{1,0:T(8,128)}, f32[768,512]{1,0:T(8,128)}, f32[3,512]{1,0:T(4,128)}) custom-call(bf16[64,768]{1,0:T(8,128)(2,1)} %refs_0_.1, bf16[128,768]{1,0:T(8,128)(2,1)} %refs_1_.1, bf16[768,512]{1,0:T(8,128)(2,1)} %refs_2_.1, bf16[3,512]{1,0:T(4,128)(2,1)} %refs_3_.1, s32[1,1,4,768]{3,2,1,0:T(4,128)} %refs_4_.1, ...), custom_call_target="tpu_custom_call" | custom-call | tf_op jit(solution)/shard_map/pallas_call | solution.py:570
  89.7 2.8 %shard_map.121 = (f32[64,512]{1,0:T(8,128)}, f32[128,512]{1,0:T(8,128)}, f32[768,512]{1,0:T(8,128)}, f32[3,512]{1,0:T(4,128)}) custom-call(f32[64,512]{1,0:T(8,128)} %get-tuple-element.12.refs_0_, f32[128,512]{1,0:T(8,128)} %get-tuple-element.13.refs_1_, f32[768,512]{1,0:T(8,128)} %get-tuple-element.14.refs_2_, f32[3,512]{1,0:T(4,128)} %get-tuple-element.15.refs_3_), custom_call_target="tpu_custom_call" | custom-call | tf_op jit(solution)/shard_map/pallas_call | solution.py:589

commit v3 on v2

--- a/solution.py
+++ b/solution.py
@@ -67,28 +67,45 @@
             copy.wait_send()
 
 
-def reduce_everywhere(place, wires, local, pair, mine, full, firsts, seconds, thirds, sums1, sums2, fill):
+def packed(value):
+    most = jnp.max(jnp.max(jnp.abs(value), axis=1, keepdims=True), axis=2, keepdims=True)
+    power = jnp.ceil(jnp.log2(jnp.maximum(most, 1e-30)) - 14.99)
+    whole = jnp.floor(value * jnp.exp2(-power) + 0.5)
+    rows = jnp.broadcast_to(power, (value.shape[0], 1, 16, 128))
+    return jnp.concatenate([whole, rows], 1).astype(jnp.int32).astype(jnp.int16)
+
+
+def unpacked(blocks):
+    wide = blocks.astype(jnp.int32).astype(F32)
+    last = blocks.shape[1] - 1
+    return wide[:, :last] * jnp.exp2(wide[:, last:])
+
+
+def reduce_everywhere(place, wires, local, pair, mine, full, firsts, seconds, thirds, sums1, sums2, sent, gathered, final, fill):
     at, k = place.at, place.at["k"]
     other = place.other_core()
     copies = []
+    for half in (0, HALF):
+        local[half + 192 : half + 200] = jnp.zeros((8, 8, 128), F32)
     fill(1 - k)
     for _, _, _, base, size in PARTS:
-        size = min(size, 196 - base)
+        size = min(size, 204 - base)
         copies.append(
             wires.send(local.at[pl.ds((1 - k) * HALF + base, size)], pair.at[pl.ds(base, size)], other)
         )
     fill(k)
-    mine[pl.ds(196, 28)] = jnp.zeros((28, 8, 128), F32)
+    mine[pl.ds(204, 20)] = jnp.zeros((20, 8, 128), F32)
     pending1 = []
     for p, (first, _, _, base, size) in enumerate(PARTS):
         copies[p].wait_recv()
-        real = min(size, 196 - base)
+        real = min(size, 204 - base)
         mine[pl.ds(base, real)] = local[pl.ds(k * HALF + base, real)] + pair[pl.ds(base, real)]
         block = size // AXIS[first]
+        sent[p][...] = packed(mine[pl.ds(base, size)].reshape(AXIS[first], block // 2, 16, 128))
         here = {}
         for apart in far_first(first):
             there, device = place.along(first, apart)
-            here[apart] = wires.send(mine.at[pl.ds(base + there * block, block)], firsts[p].at[apart], device)
+            here[apart] = wires.send(sent[p].at[there], firsts[p].at[apart], device)
         pending1.append(here)
     pending2 = []
     for p, (first, second, _, base, size) in enumerate(PARTS):
@@ -96,7 +113,7 @@
         total = mine[pl.ds(base + at[first] * block, block)]
         for apart in range(1, AXIS[first]):
             pending1[p][apart].wait_recv()
-            total = total + firsts[p][apart]
+            total = total + unpacked(firsts[p][pl.ds(apart, 1)]).reshape(block, 8, 128)
         sums1[p][...] = total
         small = block // AXIS[second]
         here = {}
@@ -138,28 +155,33 @@
         block = size // AXIS[first]
         for copy in pending4[p]:
             copy.wait_recv()
-        piece = full.at[pl.ds(k * HALF + base + at[first] * block, block)]
+        own = full[pl.ds(k * HALF + base + at[first] * block, block)].reshape(1, block // 2, 16, 128)
+        gathered[p][k, pl.ds(at[first], 1)] = packed(own)
+        piece = gathered[p].at[k, at[first]]
         pending5.append(
             {apart: wires.send(piece, piece, place.along(first, apart)[1]) for apart in far_first(first)}
         )
-        pending6.append(wires.send(piece, piece, other))
     for p, (first, second, third, base, size) in enumerate(PARTS):
-        block = size // AXIS[first]
         for apart in reversed(far_first(first)):
             pending5[p][apart].wait_recv()
-            start = lax.rem(at[first] + AXIS[first] - apart, AXIS[first])
-            piece = full.at[pl.ds(k * HALF + base + start * block, block)]
-            pending6.append(wires.send(piece, piece, other))
-    for copy in pending6:
-        copy.wait_recv()
-
-
-WIRES = 3 + 17 + 21 + 13 + 21 + 17 + 20
+        piece = gathered[p].at[k]
+        pending6.append(wires.send(piece, piece, other))
+    for turn, half in enumerate((k, 1 - k)):
+        for p, (first, second, third, base, size) in enumerate(PARTS):
+            if turn:
+                pending6[p].wait_recv()
+            final[pl.ds(half * HALF + base, size)] = unpacked(gathered[p][half]).reshape(size, 8, 128)
+
+
+WIRES = 3 + 17 + 21 + 13 + 21 + 17 + 3
 
 
 def scratch_of_reduce():
     tile = (8, 128)
-    firsts = [pltpu.VMEM((AXIS[f], n // AXIS[f]) + tile, F32) for f, s, t, _, n in PARTS]
+    coded = [(AXIS[f], n // AXIS[f] // 2 + 1, 16, 128) for f, s, t, _, n in PARTS]
+    firsts = [pltpu.VMEM(shape, jnp.int16) for shape in coded]
+    sent = [pltpu.VMEM(shape, jnp.int16) for shape in coded]
+    gathered = [pltpu.VMEM((2,) + shape, jnp.int16) for shape in coded]
     small = [n // AXIS[f] // AXIS[s] for f, s, t, _, n in PARTS]
     seconds = [pltpu.VMEM((AXIS[p[1]], m) + tile, F32) for p, m in zip(PARTS, small)]
     thirds = [pltpu.VMEM((AXIS[p[2]], m) + tile, F32) for p, m in zip(PARTS, small)]
@@ -175,6 +197,9 @@
         thirds,
         sums1,
         sums2,
+        sent,
+        gathered,
+        pltpu.VMEM((2 * HALF,) + tile, F32),
     ]
 
 
@@ -189,7 +214,7 @@
         half, low = column // 2 * HALF, column % 2
         lanes = pl.ds(column * 128, 128)
         enc_ref[:, lanes] = full[half + low * 96 : half + low * 96 + 96].reshape(768, 128)
-        rows = full[half + 192 + low * 2 : half + 194 + low * 2].reshape(16, 128)
+        rows = full[half + 200 + low * 2 : half + 202 + low * 2].reshape(16, 128)
         part = jnp.zeros((3, 128), F32)
         for group in range(4):
             part = jnp.where(g == group, rows[group * 3 : group * 3 + 3], part)
@@ -489,7 +514,7 @@
     for low in range(2):
         cut = slice(128 * low, 128 * low + 128)
         local[pl.ds(half * HALF + low * 96, 96)] = enc[:, cut].reshape(96, 8, 128)
-        local[pl.ds(half * HALF + 192 + low * 2, 2)] = rel[:, cut].reshape(2, 8, 128)
+        local[pl.ds(half * HALF + 200 + low * 2, 2)] = rel[:, cut].reshape(2, 8, 128)
 
 
 def scratch_of_meets():
@@ -545,7 +570,7 @@
     reduce_everywhere(
         place, wires, *sum_buffers, lambda half: local_sums(half, sum_buffers[0], feat_t, grads, src_part)
     )
-    tiles_out(sum_buffers[3], enc_grad, rel_grad)
+    tiles_out(sum_buffers[11], enc_grad, rel_grad)
     group.finish()
     wires.finish()
 

time: 92.6 us -> 89 us (0.961)
  Pallas kernels: 91.8 us -> 88.2 us
    pallas_call x1, Pallas kernels: 89 us -> 85.4 us  [shards(): pl.pallas_call(kernel, out_shape=tuple((jax.ShapeDtypeStruct(shape, F32)...]
where the time goes in v3:
time: 89 us; the launch traced here: 88.8 us
  Pallas kernels  88.2 us (99%)
    pallas_call x1, Pallas kernels, shards(): pl.pallas_call(kernel, out_shape=tuple((jax.ShapeDtypeStruct(shape, F32)...  85.4 us
    pallas_call x1, Pallas kernels, shards(): pl.pallas_call(hand_over, out_shape=tuple((jax.ShapeDtypeStruct(shape, F3...  2.78 us

profile of v3, /device:TPU:1, one launch (start us, length us, event | category | flops | bytes accessed | tf_op | source)
XLA Modules:
  0.0 88.8 jit_solution(8499464191126047152)
XLA Ops:
  0.6 85.4 %shard_map.120 = (f32[64,512]{1,0:T(8,128)}, f32[128,512]{1,0:T(8,128)}, f32[768,512]{1,0:T(8,128)}, f32[3,512]{1,0:T(4,128)}) custom-call(bf16[64,768]{1,0:T(8,128)(2,1)} %refs_0_.1, bf16[128,768]{1,0:T(8,128)(2,1)} %refs_1_.1, bf16[768,512]{1,0:T(8,128)(2,1)} %refs_2_.1, bf16[3,512]{1,0:T(4,128)(2,1)} %refs_3_.1, s32[1,1,4,768]{3,2,1,0:T(4,128)} %refs_4_.1, ...), custom_call_target="tpu_custom_call" | custom-call | tf_op jit(solution)/shard_map/pallas_call | solution.py:595
  86.0 2.8 %shard_map.121 = (f32[64,512]{1,0:T(8,128)}, f32[128,512]{1,0:T(8,128)}, f32[768,512]{1,0:T(8,128)}, f32[3,512]{1,0:T(4,128)}) custom-call(f32[64,512]{1,0:T(8,128)} %get-tuple-element.12.refs_0_, f32[128,512]{1,0:T(8,128)} %get-tuple-element.13.refs_1_, f32[768,512]{1,0:T(8,128)} %get-tuple-element.14.refs_2_, f32[3,512]{1,0:T(4,128)} %get-tuple-element.15.refs_3_), custom_call_target="tpu_custom_call" | custom-call | tf_op jit(solution)/shard_map/pallas_call | solution.py:614

commit v4 on v3

--- a/solution.py
+++ b/solution.py
@@ -13,7 +13,7 @@
 MESH = pl.DeviceIdType.MESH
 AXIS = {"x": 4, "y": 8, "z": 8}
 HALF = 224
-PARTS = (("z", "y", "x", 0, 64), ("y", "z", "x", 64, 64), ("x", "y", "z", 128, 96))
+PARTS = (("x", "y", "z", 128, 96), ("z", "y", "x", 0, 64), ("y", "z", "x", 64, 64))
 
 
 def far_first(axis):

time: 89 us -> 88.9 us (level)
  no operation moved by 1% of the time
where the time goes in v4:
time: 88.9 us; the launch traced here: 88.7 us
  Pallas kernels  88.1 us (99%)
    pallas_call x1, Pallas kernels, shards(): pl.pallas_call(kernel, out_shape=tuple((jax.ShapeDtypeStruct(shape, F32)...  85.3 us
    pallas_call x1, Pallas kernels, shards(): pl.pallas_call(hand_over, out_shape=tuple((jax.ShapeDtypeStruct(shape, F3...  2.78 us

profile of v4, /device:TPU:1, one launch (start us, length us, event | category | flops | bytes accessed | tf_op | source)
XLA Modules:
  0.0 88.7 jit_solution(16219921468717365605)
XLA Ops:
  0.6 85.3 %shard_map.120 = (f32[64,512]{1,0:T(8,128)}, f32[128,512]{1,0:T(8,128)}, f32[768,512]{1,0:T(8,128)}, f32[3,512]{1,0:T(4,128)}) custom-call(bf16[64,768]{1,0:T(8,128)(2,1)} %refs_0_.1, bf16[128,768]{1,0:T(8,128)(2,1)} %refs_1_.1, bf16[768,512]{1,0:T(8,128)(2,1)} %refs_2_.1, bf16[3,512]{1,0:T(4,128)(2,1)} %refs_3_.1, s32[1,1,4,768]{3,2,1,0:T(4,128)} %refs_4_.1, ...), custom_call_target="tpu_custom_call" | custom-call | tf_op jit(solution)/shard_map/pallas_call | solution.py:595
  85.9 2.8 %shard_map.121 = (f32[64,512]{1,0:T(8,128)}, f32[128,512]{1,0:T(8,128)}, f32[768,512]{1,0:T(8,128)}, f32[3,512]{1,0:T(4,128)}) custom-call(f32[64,512]{1,0:T(8,128)} %get-tuple-element.12.refs_0_, f32[128,512]{1,0:T(8,128)} %get-tuple-element.13.refs_1_, f32[768,512]{1,0:T(8,128)} %get-tuple-element.14.refs_2_, f32[3,512]{1,0:T(4,128)} %get-tuple-element.15.refs_3_), custom_call_target="tpu_custom_call" | custom-call | tf_op jit(solution)/shard_map/pallas_call | solution.py:614
